TPU v7x, 1024 devices: a whole 8x8x8 slice. The times are simulated.
1024 devices in a mesh: dp: 16 (over x, core), expert: 64 (over y, z).
Axes of the slice: x: 8, y: 8, z: 8, core: 2. Of those that a mesh axis runs over, the one named last changes fastest.
Arguments:
- out_grad: bfloat16 [16384, 7168], P('expert', 'dp'), may hold values from -6 to 6
- inputs: bfloat16 [16384, 7168], P('expert', 'dp'), may hold values from -2.5 to 2.5
- expert_ids: int32 [16384, 8], P('expert'), may hold values from 0 to 255, as said below
- gate_weights: float32 [16384, 8], P('expert'), may hold values from 0.1 to 1
- w_gate: bfloat16 [7168, 32768], P('dp', 'expert'), may hold values from -0.0625 to 0.0625
- w_up: bfloat16 [7168, 32768], P('dp', 'expert'), may hold values from -0.0625 to 0.0625
- w_down: bfloat16 [32768, 7168], P('expert', 'dp'), may hold values from -0.125 to 0.125
Outputs:
- in_grad: bfloat16 [16384, 7168], P('expert', 'dp')
- grad_gate: bfloat16 [7168, 32768], P('dp', 'expert')
- grad_up: bfloat16 [7168, 32768], P('dp', 'expert')
Inputs may be any that keep to these rules, and one draw needn't show every extreme that they name: `expert_ids`: each token names 8 different experts. Within one block of 256 consecutive tokens no expert is named by more than 12 tokens, and in every draw some expert below 16 is named by exactly 12 tokens of every block.
All inputs are finite; a program needn't handle non-finite values.
Results may differ from a plain program's by a relative error of at most 0.035.
Values may be sent and summed in bfloat16 or wider, within the bound.
A program may use at most 32 MiB of HBM per device.

v0:
```python
import jax
import jax.numpy as jnp
from jax import lax
from jax.sharding import PartitionSpec as P

HSPLIT = 4
CAP = 12


def routes(block_ids, block_gates, experts):
    flat_ids = block_ids.reshape(-1)
    matches = (flat_ids[:, None] == jnp.arange(experts, dtype=jnp.int32)[None, :]).astype(jnp.int32)
    before = jnp.cumsum(matches, axis=0) - matches
    slot_index = jnp.sum(before * matches, axis=1)
    kept_mask = jnp.sum(matches, axis=1)
    target = jnp.where(kept_mask > 0, flat_ids * CAP + slot_index, -1)
    columns = jnp.arange(experts * CAP, dtype=jnp.int32)
    hits = target[:, None] == columns[None, :]
    slot_gate = jnp.sum(jnp.where(hits, block_gates.reshape(-1)[:, None], 0.0), axis=0)
    token_of = jnp.repeat(jnp.arange(block_ids.shape[0], dtype=jnp.int32), block_ids.shape[1])
    slot_token = jnp.sum(jnp.where(hits, token_of[:, None], 0), axis=0)
    slot_used = jnp.any(hits, axis=0)
    tokens_range = jnp.arange(block_ids.shape[0], dtype=jnp.int32)
    picker = ((slot_token[:, None] == tokens_range[None, :]) & slot_used[:, None]).astype(
        jnp.bfloat16
    )
    return (picker, slot_gate, target.reshape(block_ids.shape))


def activation_grads(hidden_grad, gate_pre, up_pre):
    sigma = jax.nn.sigmoid(gate_pre)
    grad_gate_pre = (hidden_grad * up_pre * sigma * (1.0 + gate_pre * (1.0 - sigma))).astype(
        jnp.bfloat16
    )
    grad_up_pre = (hidden_grad * gate_pre * sigma).astype(jnp.bfloat16)
    return (grad_gate_pre, grad_up_pre)


def contract(left, right, left_dim, right_dim):
    return lax.dot_general(
        left, right, (((left_dim,), (right_dim,)), ((), ())), preferred_element_type=jnp.float32
    )


def per_device(out_grad, inputs, expert_ids, gate_weights, w_gate, w_up, w_down):
    devices = lax.axis_size("expert")
    experts = devices // HSPLIT
    feature_width = out_grad.shape[1]
    picker, slot_gate, target = routes(expert_ids, gate_weights, experts)
    picked_grad = jnp.dot(picker, out_grad, preferred_element_type=jnp.float32)
    sent_grad = (slot_gate[:, None] * picked_grad).astype(jnp.bfloat16)
    sent_input = jnp.dot(picker, inputs, preferred_element_type=jnp.float32).astype(jnp.bfloat16)
    sent_grad = jnp.repeat(sent_grad.reshape(experts, CAP, feature_width), HSPLIT, axis=0)
    sent_input = jnp.repeat(sent_input.reshape(experts, CAP, feature_width), HSPLIT, axis=0)
    rows_grad, rows_input = (
        lax.all_to_all(sent_grad, "expert", split_axis=0, concat_axis=0, tiled=True),
        lax.all_to_all(sent_input, "expert", split_axis=0, concat_axis=0, tiled=True),
    )
    rows_grad = rows_grad.reshape(-1, feature_width)
    rows_input = rows_input.reshape(-1, feature_width)
    down_part = contract(rows_grad, w_down, 1, 1)
    gate_part = jnp.dot(rows_input, w_gate, preferred_element_type=jnp.float32)
    up_part = jnp.dot(rows_input, w_up, preferred_element_type=jnp.float32)
    hidden_grad, gate_pre, up_pre = (
        lax.psum(down_part.astype(jnp.bfloat16), "dp").astype(jnp.float32),
        lax.psum(gate_part.astype(jnp.bfloat16), "dp").astype(jnp.float32),
        lax.psum(up_part.astype(jnp.bfloat16), "dp").astype(jnp.float32),
    )
    grad_gate_pre, grad_up_pre = activation_grads(hidden_grad, gate_pre, up_pre)
    back_part = (contract(grad_gate_pre, w_gate, 1, 1) + contract(grad_up_pre, w_up, 1, 1)).astype(
        jnp.bfloat16
    )
    grad_gate = contract(rows_input, grad_gate_pre, 0, 0).astype(jnp.bfloat16)
    grad_up = contract(rows_input, grad_up_pre, 0, 0).astype(jnp.bfloat16)
    returned = lax.all_to_all(
        back_part.reshape(devices, CAP, feature_width),
        "expert",
        split_axis=0,
        concat_axis=0,
        tiled=True,
    )
    summed = jnp.sum(
        returned.astype(jnp.float32).reshape(experts, HSPLIT, CAP, feature_width), axis=1
    )
    summed = summed.reshape(experts * CAP, feature_width)
    kept = target >= 0
    fetched = jnp.take(summed, jnp.where(kept, target, 0), axis=0)
    in_grad = jnp.sum(jnp.where(kept[:, :, None], fetched, 0.0), axis=1).astype(jnp.bfloat16)
    return (in_grad, grad_gate, grad_up)


def solution(mesh):
    placed = (
        P("expert", "dp"),
        P("expert", "dp"),
        P("expert", None),
        P("expert", None),
        P("dp", "expert"),
        P("dp", "expert"),
        P("expert", "dp"),
    )
    return jax.shard_map(
        per_device,
        mesh=mesh,
        in_specs=placed,
        out_specs=(P("expert", "dp"), P("dp", "expert"), P("dp", "expert")),
        check_vma=False,
    )
```

profile of v0, /device:TPU:113, one launch (start us, length us, event | category | flops | bytes accessed | tf_op | source)
XLA Modules:
  0.0 295.9 jit_solution(7319679293382795352)
XLA Ops:
  7.2 0.0 copy-start
  7.2 0.0 copy-start.5
  7.2 0.9 copy.32
  8.1 0.1 eq.51
  8.2 0.1 eq.55
  8.3 4.5 %reduce-window.6 = s32[16,16,128]{2,1,0:T(8,128)S(1)} reduce-window(s32[16,16,128]{2,1,0:T(8,128)S(1)} %fusion.19, s32[]{:T(128)} %constant.10.clone.1), window={size=1x1x128 pad=0_0x0_0x127_0}, to_apply=%region_1.2 | reduce-window | flops 4161536 | bytes 262148 | tf_op jit(solution)/shard_map/reduce-window
  12.9 0.4 slice_reduce_fusion
  13.3 0.2 reduce-window.9
  13.5 0.1 broadcast_add_fusion
  13.6 0.1 fusion.18
  13.7 0.3 fusion.11
  14.0 0.1 broadcast_in_dim.85
  14.1 0.2 select_reduce_fusion
  14.4 0.3 convolution_convert_fusion.5
  14.6 0.1 reshape.86
  14.7 0.0 copy-start.7
  14.7 0.0 copy-start.10
  14.7 1.1 broadcast_in_dim.89
  15.8 21.6 %all-to-all-start.1 = ((bf16[64,12,448]{2,1,0:T(8,128)(2,1)}), bf16[64,12,448]{2,1,0:T(8,128)(2,1)S(1)}, u32[]{:S(2)}, u32[]{:S(2)}) async-start(bf16[64,12,448]{2,1,0:T(8,128)(2,1)} %bitcast.2), calls=%async_computation.1 | async-start | bytes 2097152 | tf_op jit(solution)/shard_map/all_to_all | solution.py:57
  37.5 0.1 copy.38
  37.6 0.1 broadcast_in_dim.81
  37.7 0.2 select_reduce_fusion.1
  38.0 0.3 fusion.13
  38.2 0.1 reshape.83
  38.3 26.7 %all-to-all-done.1 = bf16[64,12,448]{2,1,0:T(8,128)(2,1)S(1)} async-done(((bf16[64,12,448]{2,1,0:T(8,128)(2,1)}), bf16[64,12,448]{2,1,0:T(8,128)(2,1)S(1)}, u32[]{:S(2)}, u32[]{:S(2)}) %all-to-all-start.1) | async-done | bytes 688160 | tf_op jit(solution)/shard_map/all_to_all | solution.py:57
  65.0 1.1 broadcast_in_dim.88
  66.1 8.2 %all-to-all-start = ((bf16[64,12,448]{2,1,0:T(8,128)(2,1)}), bf16[64,12,448]{2,1,0:T(8,128)(2,1)S(1)}, u32[]{:S(2)}, u32[]{:S(2)}) async-start(bf16[64,12,448]{2,1,0:T(8,128)(2,1)} %bitcast.35), calls=%async_computation | async-start | bytes 2097152 | tf_op jit(solution)/shard_map/all_to_all | solution.py:56
  74.3 0.0 all-reduce.3.cloned.1.call-start
  74.4 0.4 reshape.88
  74.8 0.0 copy-done
  74.8 0.0 copy-start.8
  74.8 1.5 convolution_convert_fusion
  76.3 1.5 convolution_convert_fusion.1
  77.7 23.6 %all-to-all-done = bf16[64,12,448]{2,1,0:T(8,128)(2,1)S(1)} async-done(((bf16[64,12,448]{2,1,0:T(8,128)(2,1)}), bf16[64,12,448]{2,1,0:T(8,128)(2,1)S(1)}, u32[]{:S(2)}, u32[]{:S(2)}) %all-to-all-start) | async-done | bytes 688160 | tf_op jit(solution)/shard_map/all_to_all | solution.py:56
  101.4 0.4 reshape.85
  101.8 2.5 convolution_convert_fusion.2
  104.2 0.0 all-reduce.3.cloned.1.call-update
  104.3 124.5 %all-reduce.3.cloned.1.call-done = (bf16[768,512]{1,0:T(8,128)(2,1)}, bf16[768,512]{1,0:T(8,128)(2,1)}, bf16[768,512]{1,0:T(8,128)(2,1)}) async-done(((bf16[768,512]{1,0:T(8,128)(2,1)}, bf16[768,512]{1,0:T(8,128)(2,1)}, bf16[768,512]{1,0:T(8,128)(2,1)}), (bf16[768,512]{1,0:T(8,128)(2,1)}, bf16[768,512]{1,0:T(8,128)(2,1)}, bf16[768,512]{1,0:T(8,128)(2,1)})) %all-reduce.3.cloned.1.call-update) | async-done | bytes 2359312 | tf_op jit(solution)/shard_map/psum | solution.py:65
  228.7 2.3 fusion.4
  231.1 0.0 copy-start.9
  231.1 0.5 fusion.26
  231.6 0.5 copy-done.1
  232.2 0.2 copy-done.3
  232.4 0.1 copy-done.9
  232.5 0.8 fusion.12
  233.4 0.3 copy.39
  233.6 1.2 reshape.89
  234.9 13.7 %all-to-all-start.2 = ((bf16[64,12,448]{2,1,0:T(8,128)(2,1)}), bf16[64,12,448]{2,1,0:T(8,128)(2,1)S(1)}, u32[]{:S(2)}, u32[]{:S(2)}) async-start(bf16[64,12,448]{2,1,0:T(8,128)(2,1)} %reshape.89), calls=%async_computation.2 | async-start | bytes 2097152 | tf_op jit(solution)/shard_map/all_to_all | solution.py:75
  248.6 0.1 reduce_sum.58
  248.7 0.1 gt.18
  248.8 0.1 copy.35
  248.9 0.1 copy.34
  249.0 0.2 copy.37
  249.2 0.2 copy.36
  249.4 0.1 copy.40
  249.5 0.1 reshape.97
  249.6 1.3 convolution_convert_fusion.4
  251.0 0.0 copy-done.4
  251.0 1.5 convolution_convert_fusion.3
  252.5 23.2 %all-to-all-done.2 = bf16[64,12,448]{2,1,0:T(8,128)(2,1)S(1)} async-done(((bf16[64,12,448]{2,1,0:T(8,128)(2,1)}), bf16[64,12,448]{2,1,0:T(8,128)(2,1)S(1)}, u32[]{:S(2)}, u32[]{:S(2)}) %all-to-all-start.2) | async-done | bytes 688160 | tf_op jit(solution)/shard_map/all_to_all | solution.py:75
  275.7 0.2 convert_reduce_fusion
  276.0 8.9 %gather_fusion = f32[2048,448]{1,0:T(8,128)} fusion(f32[192,448]{1,0:T(8,128)S(1)} %reshape.92, s32[2048]{0:T(1024)S(1)} %broadcast_clamp_fusion), kind=kCustom, calls=%fused_computation | custom fusion | bytes 7348224 | tf_op jit(solution)/shard_map/jit(_take)/gather | solution.py:87
  284.9 3.3 %fusion.1 = bf16[256,448]{1,0:T(8,128)(2,1)S(1)} fusion(f32[2048,448]{1,0:T(8,128)} %gather_fusion, pred[256,8]{1,0:T(8,128)(4,1)S(1)} %copy.37, pred[256,8]{1,0:T(8,128)(4,1)S(1)} %copy.36), kind=kLoop, calls=%fused_computation.3 | loop fusion | flops 2637824 | bytes 3903488 | tf_op jit(solution)/shard_map/reduce_sum | solution.py:88
  288.2 0.8 copy.41
  (17 shorter events, 0.1 us)
Async XLA Ops:
  7.2 67.6 %copy-start = (bf16[448,512]{1,0:T(8,128)(2,1)S(1)}, bf16[448,512]{1,0:T(8,128)(2,1)}, u32[]{:S(2)}) copy-start(bf16[448,512]{1,0:T(8,128)(2,1)} %param.11) | copy-start | bytes 1376260
  7.2 7.2 %copy-start.5 = (bf16[256,448]{0,1:T(8,128)(2,1)S(1)}, bf16[256,448]{0,1:T(8,128)(2,1)}, u32[]{:S(2)}) copy-start(bf16[256,448]{0,1:T(8,128)(2,1)} %param.8) | copy-start | bytes 688132
  14.7 22.8 %copy-start.7 = (f32[256,8]{0,1:T(8,128)S(1)}, f32[256,8]{0,1:T(8,128)}, u32[]{:S(2)}) copy-start(f32[256,8]{0,1:T(8,128)} %param.10) | copy-start | bytes 24580
  14.7 23.3 %copy-start.10 = (bf16[256,448]{0,1:T(8,128)(2,1)S(1)}, bf16[256,448]{0,1:T(8,128)(2,1)}, u32[]{:S(2)}) copy-start(bf16[256,448]{0,1:T(8,128)(2,1)} %param.7) | copy-start | bytes 688132
  15.8 49.1 %all-to-all-start.1 = ((bf16[64,12,448]{2,1,0:T(8,128)(2,1)}), bf16[64,12,448]{2,1,0:T(8,128)(2,1)S(1)}, u32[]{:S(2)}, u32[]{:S(2)}) async-start(bf16[64,12,448]{2,1,0:T(8,128)(2,1)} %bitcast.2), calls=%async_computation.1 | async-start | bytes 2097152 | tf_op jit(solution)/shard_map/all_to_all | solution.py:57
  66.1 35.3 %all-to-all-start = ((bf16[64,12,448]{2,1,0:T(8,128)(2,1)}), bf16[64,12,448]{2,1,0:T(8,128)(2,1)S(1)}, u32[]{:S(2)}, u32[]{:S(2)}) async-start(bf16[64,12,448]{2,1,0:T(8,128)(2,1)} %bitcast.35), calls=%async_computation | async-start | bytes 2097152 | tf_op jit(solution)/shard_map/all_to_all | solution.py:56
  74.3 154.4 %all-reduce.3.cloned.1.call-start = ((), (), s32[]{:S(2)}) async-start(), calls=%async_computation.3 | async-start | bytes 4718592 | tf_op jit(solution)/shard_map/psum | solution.py:65
  74.8 1.5 copy-start.8
  231.1 1.1 copy-start.1
  231.1 1.4 copy-start.3
  231.1 1.5 copy-start.9
  234.9 14.1 %copy-start.6 = (s32[256,8]{0,1:T(8,128)S(1)}, s32[256,8]{0,1:T(8,128)}, u32[]{:S(2)}) copy-start(s32[256,8]{0,1:T(8,128)} %param.9) | copy-start | bytes 24580
  234.9 40.9 %all-to-all-start.2 = ((bf16[64,12,448]{2,1,0:T(8,128)(2,1)}), bf16[64,12,448]{2,1,0:T(8,128)(2,1)S(1)}, u32[]{:S(2)}, u32[]{:S(2)}) async-start(bf16[64,12,448]{2,1,0:T(8,128)(2,1)} %reshape.89), calls=%async_computation.2 | async-start | bytes 2097152 | tf_op jit(solution)/shard_map/all_to_all | solution.py:75
  249.6 1.4 copy-start.2
  249.6 1.4 copy-start.4
Sparse Core Ops, SparseCore 0:
  104.4 124.3 all-reduce.2
where the time goes:
time: 302 us; the launch traced here: 296 us
  waiting for transfers between devices  198 us (66%)
  starting transfers between devices  43.6 us (14%)
  local copies, waits for them, and re-layouts  18.2 us (6%)
  between operations  14.4 us (5%)
  other arithmetic  11.6 us (4%)
  matrix products  10.1 us (3%)
    psum x1, waiting for transfers between devices, per_device(): lax.psum(down_part.astype(jnp.bfloat16), 'dp').astype(jnp.float32)  124 us
    all_to_all x1, waiting for transfers between devices, per_device(): lax.all_to_all(sent_input, 'expert', split_axis=0, concat_axis=0, tiled=T...  26.7 us
    all_to_all x1, waiting for transfers between devices, per_device(): lax.all_to_all(sent_grad, 'expert', split_axis=0, concat_axis=0, tiled=True)  23.6 us
    all_to_all x1, waiting for transfers between devices, per_device(): lax.all_to_all(back_part.reshape(devices, CAP, feature_width), 'expert',...  23.2 us
    all_to_all x1, starting transfers between devices, per_device(): lax.all_to_all(sent_input, 'expert', split_axis=0, concat_axis=0, tiled=T...  21.6 us
    all_to_all x1, starting transfers between devices, per_device(): lax.all_to_all(back_part.reshape(devices, CAP, feature_width), 'expert',...  13.7 us
    gather x1, local copies, waits for them, and re-layouts, per_device(): fetched = jnp.take(summed, jnp.where(kept, target, 0), axis=0)  8.91 us
    all_to_all x1, starting transfers between devices, per_device(): lax.all_to_all(sent_grad, 'expert', split_axis=0, concat_axis=0, tiled=True)  8.24 us
  transfers between devices with their start and end apart: 4, of which 4 were waited for; matrix products, arithmetic and copies ran while one was open for 3% of the time, Pallas kernels for 0%

commit v1 on v0

v1 whole, which is shorter than its diff:
```python
import functools

import jax
import jax.numpy as jnp
from jax import lax
from jax.experimental import pallas as pl
from jax.experimental.pallas import tpu as pltpu
from jax.sharding import PartitionSpec as P

HSPLIT = 4
CAP = 12
SLOT = 16
CORES = 2
BF = jnp.bfloat16
F32 = jnp.float32


def grid_of(devices):
    side = 1
    while side * side < devices:
        side *= 2
    return devices // side, side


def mm(a, b):
    return lax.dot_general(a, b, (((1,), (0,)), ((), ())), preferred_element_type=F32)


def mm_nt(a, b):
    return lax.dot_general(a, b, (((1,), (1,)), ((), ())), preferred_element_type=F32)


def mm_tn(a, b):
    return lax.dot_general(a, b, (((0,), (0,)), ((), ())), preferred_element_type=F32)


def iota(shape, dim):
    return lax.broadcasted_iota(jnp.int32, shape, dim)


def near_first(n):
    order = []
    for k in range(1, n // 2 + 1):
        order.append(k)
        if n - k != k:
            order.append(n - k)
    return order


def kernel(
    sizes,
    out_grad,
    inputs,
    ids,
    gates,
    w_gate,
    w_up,
    w_down,
    in_grad,
    grad_gate,
    grad_up,
    picker_t,
    ysend,
    yrecv,
    zsend,
    rows,
    csend,
    crecv,
    own,
    rsend,
    rrecv,
    acts,
    back,
    zret,
    yback,
    yret,
    y_ss,
    y_rs,
    z_ss,
    z_rs,
    c_ss,
    c_rs,
    r_ss,
    r_rs,
    a_ss,
    a_rs,
    s_ss,
    s_rs,
    b_ss,
    b_rs,
    e_ss,
    e_rs,
):
    nx, ny, nz = sizes
    groups = nz // HSPLIT
    blk = groups * SLOT
    slots = ny * blk
    per_z = ny * CAP
    tokens = out_grad.shape[0]
    half = w_gate.shape[1] // CORES

    dp = lax.axis_index("dp")
    ex = lax.axis_index("expert")
    x, core = dp // CORES, dp % CORES
    y, z = ex // nz, ex % nz
    zgroup = z // HSPLIT
    sibling = (x * CORES + 1 - core, ex)

    def at_y(k):
        t = (y + k) % ny
        return t, (dp, t * nz + z)

    def at_z(k):
        t = (z + k) % nz
        return t, (dp, y * nz + t)

    def at_x(k):
        t = (x + k) % nx
        return t, (t * CORES + core, ex)

    def remote(src, dst, ssem, rsem, device):
        return pltpu.make_async_remote_copy(
            src_ref=src,
            dst_ref=dst,
            send_sem=ssem,
            recv_sem=rsem,
            device_id=device,
            device_id_type=pl.DeviceIdType.MESH,
        )

    partners = (
        [at_y(k)[1] for k in range(1, ny)]
        + [at_z(k)[1] for k in range(1, nz)]
        + [at_x(k)[1] for k in range(1, nx)]
        + [sibling]
    )
    barrier = pltpu.get_barrier_semaphore()
    for device in partners:
        pl.semaphore_signal(barrier, inc=1, device_id=device, device_id_type=pl.DeviceIdType.MESH)

    lane = iota((tokens, 128), 1)
    hits = jnp.zeros((tokens, 128), F32)
    gate = jnp.zeros((tokens, 128), F32)
    for k in range(ids.shape[1]):
        hit = ids[:, k : k + 1] == lane
        hits = hits + jnp.where(hit, 1.0, 0.0)
        gate = gate + jnp.where(hit, gates[:, k : k + 1], 0.0)
    hits_b = hits.astype(BF)
    before = jnp.where(iota((tokens, tokens), 0) > iota((tokens, tokens), 1), 1.0, 0.0).astype(BF)
    slot_of = mm(before, hits_b).astype(BF)
    expand = jnp.where(iota((slots, 128), 0) // SLOT == iota((slots, 128), 1), 1.0, 0.0).astype(BF)
    hit_rt = mm_nt(expand, hits_b)
    slot_rt = mm_nt(expand, slot_of)
    wanted = (iota((slots, tokens), 0) % SLOT).astype(F32)
    picker = jnp.where(jnp.logical_and(hit_rt > 0.5, slot_rt == wanted), 1.0, 0.0)
    gate_1 = gate.astype(BF)
    rest = gate - gate_1.astype(F32)
    gate_2 = rest.astype(BF)
    gate_3 = (rest - gate_2.astype(F32)).astype(BF)
    gate_rt = mm_nt(expand, gate_1) + mm_nt(expand, gate_2) + mm_nt(expand, gate_3)
    scale = jnp.sum(picker * gate_rt, axis=1, keepdims=True)
    picker_b = picker.astype(BF)
    hit_tr = mm_nt(hits_b, expand)
    slot_tr = mm_nt(slot_of, expand)
    wanted_t = (iota((tokens, slots), 1) % SLOT).astype(F32)
    picker_t[...] = jnp.where(
        jnp.logical_and(hit_tr > 0.5, slot_tr == wanted_t), 1.0, 0.0
    ).astype(BF)

    def block(ref, index, count, *lead):
        return ref.at[(*lead, pl.ds(pl.multiple_of(index * count, 16), count))]

    def y_copies(a, source, target, ss, rs):
        copies = {}
        for k in near_first(ny):
            t, device = at_y(k)
            copies[k] = remote(
                block(source, t, blk, a),
                block(target, y, blk, a),
                ss.at[a, k],
                rs.at[a, k],
                device,
            )
        return copies

    ysend[0] = mm(picker_b, inputs[...]).astype(BF)
    pl.semaphore_wait(barrier, len(partners))
    y_in = y_copies(0, ysend, yrecv, y_ss, y_rs)
    for copy in y_in.values():
        copy.start()
    ysend[1] = (scale * mm(picker_b, out_grad[...])).astype(BF)
    y_gr = y_copies(1, ysend, yrecv, y_ss, y_rs)
    for copy in y_gr.values():
        copy.start()

    col = iota((groups * per_z, slots), 1)
    seat = (col // SLOT % groups) * per_z + (col // blk) * CAP + col % SLOT
    pack = jnp.where(
        jnp.logical_and(seat == iota((groups * per_z, slots), 0), col % SLOT < CAP), 1.0, 0.0
    ).astype(BF)
    row = iota((slots, groups * per_z), 0)
    seat_t = (row // SLOT % groups) * per_z + (row // blk) * CAP + row % SLOT
    unpack = jnp.where(
        jnp.logical_and(seat_t == iota((slots, groups * per_z), 1), row % SLOT < CAP), 1.0, 0.0
    ).astype(BF)

    def z_phase(a, y_in_flight):
        here = pl.ds(pl.multiple_of(y * blk, 16), blk)
        yrecv[a, here] = ysend[a, here]
        for copy in y_in_flight.values():
            copy.wait_recv()
        zsend[a] = mm(pack, yrecv[a]).astype(BF)
        copies = {}
        for k in near_first(nz):
            t, device = at_z(k)
            copies[k] = remote(
                block(zsend, t // HSPLIT, per_z, a),
                block(rows, z, per_z, a),
                z_ss.at[a, k],
                z_rs.at[a, k],
                device,
            )
            copies[k].start()
        rows[a, pl.ds(pl.multiple_of(z * per_z, 16), per_z)] = zsend[
            a, pl.ds(pl.multiple_of(zgroup * per_z, 16), per_z)
        ]
        return copies

    total = nz * per_z
    chunk = total // 2

    def product(a, w, out, mine, transposed):
        which = core if mine else 1 - core
        start = pl.multiple_of(which * half, 128)

        def body(i, _):
            at = pl.ds(pl.multiple_of(i * chunk, 16), chunk)
            left = rows[a, at]
            if transposed:
                value = mm_nt(left, w[pl.ds(start, half), :])
            else:
                value = mm(left, w[:, pl.ds(start, half)])
            out[at] = value.astype(out.dtype)
            return 0

        lax.fori_loop(0, 2, body, 0)

    def cores_start(n):
        copy = remote(csend.at[n], crecv.at[n], c_ss.at[n], c_rs.at[n], sibling)
        copy.start()
        return copy

    shard = total // nx

    def x_scatter(n, core_copy):
        core_copy.wait_recv()

        def body(i, _):
            at = pl.ds(pl.multiple_of(i * shard, 16), shard)
            value = own[n, at] + crecv[n, at].astype(F32)
            own[n, at] = value
            rsend[n, at] = value.astype(BF)
            return 0

        lax.fori_loop(0, nx, body, 0)
        copies = {}
        for k in near_first(nx):
            t, device = at_x(k)
            copies[k] = remote(
                block(rsend, t, shard, n),
                block(rrecv, x, shard, n),
                r_ss.at[n, k],
                r_rs.at[n, k],
                device,
            )
            copies[k].start()
        return copies

    z_in = z_phase(0, y_in)
    for copy in z_in.values():
        copy.wait_recv()
    z_gr = z_phase(1, y_gr)

    product(0, w_gate, csend.at[0], False, False)
    c_gate = cores_start(0)
    product(0, w_up, csend.at[1], False, False)
    c_up = cores_start(1)
    product(0, w_gate, own.at[0], True, False)
    r_gate = x_scatter(0, c_gate)
    product(0, w_up, own.at[1], True, False)
    r_up = x_scatter(1, c_up)

    for copy in z_gr.values():
        copy.wait_recv()
    product(1, w_down, csend.at[2], False, True)
    c_down = cores_start(2)
    product(1, w_down, own.at[2], True, True)
    r_down = x_scatter(2, c_down)

    mine = pl.ds(pl.multiple_of(x * shard, 16), shard)

    def x_sum(n, copies):
        value = own[n, mine]
        for k in copies:
            copies[k].wait_recv()
        for k in copies:
            source = (x + nx - k) % nx
            value = value + rrecv[n, pl.ds(pl.multiple_of(source * shard, 16), shard)].astype(F32)
        return value

    gate_pre = x_sum(0, r_gate)
    up_pre = x_sum(1, r_up)
    sigma = 1.0 / (1.0 + jnp.exp(-gate_pre))
    gate_factor = up_pre * sigma * (1.0 + gate_pre * (1.0 - sigma))
    up_factor = gate_pre * sigma
    hidden_grad = x_sum(2, r_down)
    acts[core, mine] = (hidden_grad * gate_factor).astype(BF)
    acts[CORES + core, mine] = (hidden_grad * up_factor).astype(BF)

    def to_sibling(a, k):
        source = (x + nx - k) % nx
        view = block(acts, source, shard, a * CORES + core)
        return remote(view, view, s_ss.at[a, k], s_rs.at[a, k], sibling)

    gathers = []
    for k in near_first(nx):
        for a in range(2):
            _, device = at_x(k)
            view = block(acts, x, shard, a * CORES + core)
            copy = remote(view, view, a_ss.at[a, k], a_rs.at[a, k], device)
            copy.start()
            gathers.append((a, k, copy))
    forwards = []
    for a in range(2):
        copy = to_sibling(a, 0)
        copy.start()
        forwards.append(copy)
    for a, k, copy in gathers:
        copy.wait_recv()
        copy = to_sibling(a, k)
        copy.start()
        forwards.append(copy)
    for copy in forwards:
        copy.wait_recv()

    def back_body(i, _):
        at = pl.ds(pl.multiple_of(i * chunk, 16), chunk)
        value = None
        for a, w in ((0, w_gate), (1, w_up)):
            for c in range(CORES):
                term = mm_nt(acts[a * CORES + c, at], w[:, c * half : (c + 1) * half])
                value = term if value is None else value + term
        back[at] = value.astype(BF)
        return 0

    lax.fori_loop(0, 2, back_body, 0)

    z_back = {}
    for k in near_first(nz):
        t, device = at_z(k)
        z_back[k] = remote(
            block(back, t, per_z), block(zret, z, per_z), b_ss.at[k], b_rs.at[k], device
        )
        z_back[k].start()
    at_mine = pl.ds(pl.multiple_of(z * per_z, 16), per_z)
    zret[at_mine] = back[at_mine]

    for a, grad in ((0, grad_gate), (1, grad_up)):
        for c in range(CORES):
            grad[:, c * half : (c + 1) * half] = mm_tn(rows[0], acts[a * CORES + c]).astype(BF)

    for copy in z_back.values():
        copy.wait_recv()
    sums = []
    for g in range(groups):
        value = None
        for q in range(HSPLIT):
            first = (g * HSPLIT + q) * per_z
            term = zret[first : first + per_z].astype(F32)
            value = term if value is None else value + term
        sums.append(value.astype(BF))
    spread = None
    for g in range(groups):
        term = mm(unpack[:, g * per_z : (g + 1) * per_z], sums[g])
        spread = term if spread is None else spread + term
    yback[...] = spread.astype(BF)
    y_back = {}
    for k in near_first(ny):
        t, device = at_y(k)
        y_back[k] = remote(block(yback, t, blk), block(yret, y, blk), e_ss.at[k], e_rs.at[k], device)
        y_back[k].start()
    here = pl.ds(pl.multiple_of(y * blk, 16), blk)
    yret[here] = yback[here]
    for copy in y_back.values():
        copy.wait_recv()
    in_grad[...] = mm(picker_t[...], yret[...]).astype(BF)

    for copies in (y_in, y_gr, z_in, z_gr, r_gate, r_up, r_down, z_back, y_back):
        for copy in copies.values():
            copy.wait_send()
    for copy in (c_gate, c_up, c_down):
        copy.wait_send()
    for _, _, copy in gathers:
        copy.wait_send()
    for copy in forwards:
        copy.wait_send()


def per_device(sizes, out_grad, inputs, expert_ids, gate_weights, w_gate, w_up, w_down):
    nx, ny, nz = sizes
    tokens, feature = out_grad.shape
    hidden = w_gate.shape[1]
    half = hidden // CORES
    groups = nz // HSPLIT
    slots = ny * groups * SLOT
    per_z = ny * CAP
    total = nz * per_z
    dma = pltpu.SemaphoreType.DMA
    vmem = pltpu.VMEM
    return pl.pallas_call(
        functools.partial(kernel, sizes),
        out_shape=(
            jax.ShapeDtypeStruct((tokens, feature), BF),
            jax.ShapeDtypeStruct((feature, hidden), BF),
            jax.ShapeDtypeStruct((feature, hidden), BF),
        ),
        in_specs=[pl.BlockSpec(memory_space=vmem)] * 7,
        out_specs=(pl.BlockSpec(memory_space=vmem),) * 3,
        scratch_shapes=[
            vmem((tokens, slots), BF),
            vmem((2, slots, feature), BF),
            vmem((2, slots, feature), BF),
            vmem((2, groups * per_z, feature), BF),
            vmem((2, total, feature), BF),
            vmem((3, total, half), BF),
            vmem((3, total, half), BF),
            vmem((3, total, half), F32),
            vmem((3, total, half), BF),
            vmem((3, total, half), BF),
            vmem((2 * CORES, total, half), BF),
            vmem((total, feature), BF),
            vmem((total, feature), BF),
            vmem((slots, feature), BF),
            vmem((slots, feature), BF),
            dma((2, ny)),
            dma((2, ny)),
            dma((2, nz)),
            dma((2, nz)),
            dma((3,)),
            dma((3,)),
            dma((3, nx)),
            dma((3, nx)),
            dma((2, nx)),
            dma((2, nx)),
            dma((2, nx)),
            dma((2, nx)),
            dma((nz,)),
            dma((nz,)),
            dma((ny,)),
            dma((ny,)),
        ],
        compiler_params=pltpu.CompilerParams(
            collective_id=0, has_side_effects=True, vmem_limit_bytes=48 * 1024 * 1024
        ),
        cost_estimate=pl.CostEstimate(
            flops=14 * total * feature * hidden, bytes_accessed=4_000_000, transcendentals=0
        ),
    )(out_grad, inputs, expert_ids, gate_weights, w_gate, w_up, w_down)


def solution(mesh, sizes=None):
    if sizes is None:
        ny, nz = grid_of(mesh.shape["expert"])
        sizes = (mesh.shape["dp"] // CORES, ny, nz)
    placed = (
        P("expert", "dp"),
        P("expert", "dp"),
        P("expert", None),
        P("expert", None),
        P("dp", "expert"),
        P("dp", "expert"),
        P("expert", "dp"),
    )
    return jax.shard_map(
        functools.partial(per_device, sizes),
        mesh=mesh,
        in_specs=placed,
        out_specs=(P("expert", "dp"), P("dp", "expert"), P("dp", "expert")),
        check_vma=False,
    )
```

time: 302 us -> 142 us (0.47)
  the two profiles are of different devices: /device:TPU:113 before, /device:TPU:11 now
where the time goes in v1:
time: 142 us
  Pallas kernels  136 us (96%)
  local copies, waits for them, and re-layouts  5.53 us (4%)
    pallas_call x1, Pallas kernels, per_device(): pl.pallas_call(functools.partial(kernel, sizes), out_shape=(jax.ShapeDtyp...  136 us
    unnamed x19, local copies, waits for them, and re-layouts  4.7 us

profile of v1, /device:TPU:11, one launch (start us, length us, event | category | flops | bytes accessed | tf_op | source)
XLA Modules:
  0.0 141.9 jit_solution(5101389583859658408)
XLA Ops:
  0.6 0.0 copy-start.5
  0.6 0.0 copy-start.3
  0.7 0.9 copy.12.ids
  1.5 0.0 copy-done.5
  1.5 0.0 copy-start.4
  1.5 0.1 copy.13.gates
  1.7 0.0 copy-done.3
  1.7 0.0 copy-start.2
  1.7 0.1 copy.10.out_grad
  1.8 0.7 copy-done.4
  2.5 0.1 copy.11.inputs
  2.6 0.1 copy-done.2
  2.7 0.0 copy-start
  2.7 0.0 copy-start.1
  2.7 0.2 copy.14.w_down
  2.9 0.8 copy-done
  3.7 0.1 copy-done.1
  3.9 135.6 %shard_map.94 = (bf16[256,448]{1,0:T(8,128)(2,1)S(1)}, bf16[448,512]{1,0:T(8,128)(2,1)S(1)}, bf16[448,512]{1,0:T(8,128)(2,1)S(1)}) custom-call(bf16[256,448]{1,0:T(8,128)(2,1)S(1)} %copy.10.out_grad, bf16[256,448]{1,0:T(8,128)(2,1)S(1)} %copy.11.inputs, s32[256,8]{1,0:T(8,128)S(1)} %copy.12.ids, f32[256,8]{1,0:T(8,128)S(1)} %copy.13.gates, ...), custom_call_target="tpu_custom_call" | custom-call | flops 2466250752 | bytes 4000000 | tf_op jit(solution)/shard_map/pallas_call | solution.py:420
  139.5 0.8 copy.15
  140.3 0.8 copy.18
  141.1 0.8 copy.19
Async XLA Ops:
  0.6 0.9 copy-start.5
  0.6 1.0 copy-start.3
  1.5 1.0 copy-start.4
  1.7 1.0 copy-start.2
  2.7 1.0 copy-start
  2.7 1.2 copy-start.1

commit v2 on v1

v2 whole, which is shorter than its diff:
```python
import functools

import jax
import jax.numpy as jnp
from jax import lax
from jax.experimental import pallas as pl
from jax.experimental.pallas import tpu as pltpu
from jax.sharding import PartitionSpec as P

HSPLIT = 4
CAP = 12
SLOT = 16
PARTS = (48, 48)
CHUNKS = len(PARTS)
Z_FIRST = (
    ((0, 1), (1, 1), (1, 3)),
    ((0, 2), (1, 3), (1, 0), (0, 0)),
    ((0, 1), (1, 0), (1, 3), (0, 3)),
    ((0, 2), (1, 2), (1, 0)),
)
Z_SECOND = (
    ((7, 1), (6, 1), (5, 1)),
    ((0, 3), (0, 2), (4, 0), (2, 0)),
    ((3, 0), (3, 1), (7, 3), (1, 3)),
    ((4, 2), (5, 2), (6, 2)),
)
CORES = 2
BF = jnp.bfloat16
F32 = jnp.float32


def grid_of(devices):
    side = 1
    while side * side < devices:
        side *= 2
    return devices // side, side


def mm(a, b):
    return lax.dot_general(a, b, (((1,), (0,)), ((), ())), preferred_element_type=F32)


def mm_nt(a, b):
    return lax.dot_general(a, b, (((1,), (1,)), ((), ())), preferred_element_type=F32)


def mm_tn(a, b):
    return lax.dot_general(a, b, (((0,), (0,)), ((), ())), preferred_element_type=F32)


def iota(shape, dim):
    return lax.broadcasted_iota(jnp.int32, shape, dim)


def near_first(n):
    order = []
    for k in range(1, n // 2 + 1):
        order.append(k)
        if n - k != k:
            order.append(n - k)
    return order


def kernel(
    sizes,
    out_grad_t,
    inputs_t,
    ids_t,
    gates_t,
    w_gate,
    w_up,
    w_down_t,
    in_grad_t,
    grad_gate,
    grad_up,
    pick,
    ysend,
    yrecv,
    zsend,
    rows,
    csend,
    crecv,
    own,
    rsend,
    rrecv,
    xcomb,
    acts,
    back,
    zret,
    yback,
    yret,
    y_ss,
    y_rs,
    z_ss,
    z_rs,
    c_ss,
    c_rs,
    r_ss,
    r_rs,
    a_ss,
    a_rs,
    s_ss,
    s_rs,
    b_ss,
    b_rs,
    e_ss,
    e_rs,
):
    nx, ny, nz = sizes
    groups = nz // HSPLIT
    blk = groups * SLOT
    slots = ny * blk
    per_z = ny * CAP
    tokens = ids_t.shape[1]
    half = w_gate.shape[1] // CORES

    dp = lax.axis_index("dp")
    ex = lax.axis_index("expert")
    x, core = dp // CORES, dp % CORES
    y, z = ex // nz, ex % nz
    zgroup = z // HSPLIT
    sibling = (x * CORES + 1 - core, ex)

    def at_y(k):
        t = (y + k) % ny
        return t, (dp, t * nz + z)

    def at_z(k):
        t = (z + k) % nz
        return t, (dp, y * nz + t)

    def at_x(k):
        t = (x + k) % nx
        return t, (t * CORES + core, ex)

    def remote(src, dst, ssem, rsem, device):
        return pltpu.make_async_remote_copy(
            src_ref=src,
            dst_ref=dst,
            send_sem=ssem,
            recv_sem=rsem,
            device_id=device,
            device_id_type=pl.DeviceIdType.MESH,
        )

    partners = (
        [at_y(k)[1] for k in range(1, ny)]
        + [at_z(k)[1] for k in range(1, nz)]
        + [at_x(k)[1] for k in range(1, nx)]
        + [sibling]
    )
    barrier = pltpu.get_barrier_semaphore()
    for device in partners:
        pl.semaphore_signal(barrier, inc=1, device_id=device, device_id_type=pl.DeviceIdType.MESH)

    expert = iota((128, tokens), 0)
    hits = jnp.zeros((128, tokens), F32)
    gate = jnp.zeros((128, tokens), F32)
    for k in range(ids_t.shape[0]):
        hit = ids_t[k : k + 1, :] == expert
        hits = hits + jnp.where(hit, 1.0, 0.0)
        gate = gate + jnp.where(hit, gates_t[k : k + 1, :], 0.0)
    hits_b = hits.astype(BF)
    before = jnp.where(iota((tokens, tokens), 0) < iota((tokens, tokens), 1), 1.0, 0.0).astype(BF)
    slot_of = mm(hits_b, before).astype(BF)
    expand = jnp.where(iota((slots, 128), 0) // SLOT == iota((slots, 128), 1), 1.0, 0.0).astype(BF)
    hit_rt = mm(expand, hits_b)
    slot_rt = mm(expand, slot_of)
    wanted = (iota((slots, tokens), 0) % SLOT).astype(F32)
    picker = jnp.where(jnp.logical_and(hit_rt > 0.5, slot_rt == wanted), 1.0, 0.0)
    picker_b = picker.astype(BF)
    pick[...] = picker_b

    def block(ref, index, count, *lead):
        return ref.at[(*lead, pl.ds(pl.multiple_of(index * count, 16), count))]

    def y_copies(a):
        copies = {}
        for k in near_first(ny):
            t, device = at_y(k)
            copies[k] = remote(
                block(ysend, t, blk, a),
                block(yrecv, y, blk, a),
                y_ss.at[a, k],
                y_rs.at[a, k],
                device,
            )
            copies[k].start()
        return copies

    ysend[0] = mm_nt(picker_b, inputs_t[...]).astype(BF)
    pl.semaphore_wait(barrier, len(partners))
    y_in = y_copies(0)
    gate_1 = gate.astype(BF)
    rest = gate - gate_1.astype(F32)
    gate_2 = rest.astype(BF)
    gate_3 = (rest - gate_2.astype(F32)).astype(BF)
    gate_rt = mm(expand, gate_1) + mm(expand, gate_2) + mm(expand, gate_3)
    scale = jnp.sum(picker * gate_rt, axis=1, keepdims=True)
    ysend[1] = (scale * mm_nt(picker_b, out_grad_t[...])).astype(BF)
    y_gr = y_copies(1)

    col = iota((groups * per_z, slots), 1)
    seat = (col // SLOT % groups) * per_z + (col // blk) * CAP + col % SLOT
    pack = jnp.where(
        jnp.logical_and(seat == iota((groups * per_z, slots), 0), col % SLOT < CAP), 1.0, 0.0
    ).astype(BF)
    row = iota((slots, groups * per_z), 0)
    seat_t = (row // SLOT % groups) * per_z + (row // blk) * CAP + row % SLOT
    unpack = jnp.where(
        jnp.logical_and(seat_t == iota((slots, groups * per_z), 1), row % SLOT < CAP), 1.0, 0.0
    ).astype(BF)

    def arrived(copies):
        for copy in copies.values():
            copy.wait_recv()

    def pack_rows(a, y_in_flight):
        here = pl.ds(pl.multiple_of(y * blk, 16), blk)
        yrecv[a, here] = ysend[a, here]
        arrived(y_in_flight)
        packed = mm(pack, yrecv[a]).astype(BF)
        for g in range(groups):
            for ch in range(CHUNKS):
                first = g * per_z + starts[ch]
                zsend[(a * CHUNKS + ch) * groups + g, : PARTS[ch]] = packed[
                    first : first + PARTS[ch]
                ]

    place = z % HSPLIT

    def z_device(other, to):
        group = 1 - zgroup if other else zgroup
        return (dp, y * nz + group * HSPLIT + to)

    def z_rows(n, ch, source):
        return block(rows, source, PARTS[ch], n)

    def z_source(tag):
        group = 1 - zgroup if tag >= HSPLIT else zgroup
        return group * HSPLIT + tag % HSPLIT

    def z_first(n, ch, at, j):
        other, to = Z_FIRST[at][j]
        group = 1 - zgroup if other else zgroup
        tag = at + HSPLIT * other
        return remote(
            zsend.at[n * groups + group, pl.ds(0, PARTS[ch])],
            z_rows(n, ch, z),
            z_ss.at[n, j],
            z_rs.at[n, tag],
            z_device(other, to),
        )

    def z_second(n, ch, at, j):
        tag, to = Z_SECOND[at][j]
        view = z_rows(n, ch, z_source(tag))
        return remote(view, view, z_ss.at[n, 4 + j], z_rs.at[n, tag], z_device(False, to))

    def z_arrival(n, ch, tag):
        view = z_rows(n, ch, z_source(tag))
        remote(view, view, z_ss.at[n, 0], z_rs.at[n, tag], sibling).wait_recv()

    def each_place(step):
        for at in range(HSPLIT):
            pl.when(place == at)(functools.partial(step, at))

    def z_start(a, ch):
        n = a * CHUNKS + ch
        part = PARTS[ch]

        def step(at):
            for j in range(len(Z_FIRST[at])):
                z_first(n, ch, at, j).start()

        each_place(step)
        rows[n, pl.ds(pl.multiple_of(z * part, 16), part)] = zsend[n * groups + zgroup, :part]

    def z_pass(a, ch):
        n = a * CHUNKS + ch

        def step(at):
            done = []
            for j, (tag, _) in enumerate(Z_SECOND[at]):
                if tag not in done:
                    z_arrival(n, ch, tag)
                    done.append(tag)
                z_second(n, ch, at, j).start()

        each_place(step)

    def z_finish(a, ch):
        n = a * CHUNKS + ch

        def step(at):
            passed = [tag for tag, _ in Z_SECOND[at]]
            for tag in range(nz):
                if tag != at and tag not in passed:
                    z_arrival(n, ch, tag)

        each_place(step)

    def z_sent(n, ch):
        def step(at):
            for j in range(len(Z_FIRST[at])):
                z_first(n, ch, at, j).wait_send()
            for j in range(len(Z_SECOND[at])):
                z_second(n, ch, at, j).wait_send()

        each_place(step)

    def product(a, ch, w, mine):
        start = pl.multiple_of((core if mine else 1 - core) * half, 128)
        return mm(rows[a * CHUNKS + ch, : nz * PARTS[ch]], w[:, pl.ds(start, half)])

    def cores_send(p, ch, a, w):
        n = p * CHUNKS + ch
        total = nz * PARTS[ch]
        csend[n, :total] = product(a, ch, w, False).astype(BF)
        at = pl.ds(0, total)
        copy = remote(csend.at[n, at], crecv.at[n, at], c_ss.at[n], c_rs.at[n], sibling)
        copy.start()
        return copy

    def shard_at(ch, k):
        shard = nz * PARTS[ch] // nx
        return pl.ds(pl.multiple_of((x + nx + k) % nx * shard, 16), shard)

    def x_copy(n, ch, role, source, k):
        where = pl.ds(0, nz * PARTS[ch] // nx)
        return remote(
            source, rrecv.at[n, role, where], r_ss.at[n, role], r_rs.at[n, role], at_x(k + nx)[1]
        )

    def x_scatter(p, ch, a, w, core_copy):
        n = p * CHUNKS + ch
        total = nz * PARTS[ch]
        value = product(a, ch, w, True)
        core_copy.wait_recv()
        value = value + crecv[n, :total].astype(F32)
        own[n, :total] = value
        rsend[n, :total] = value.astype(BF)
        copies = {}
        if nx > 1:
            far = 2 if (p + ch) % 2 == 0 else -2
            for role, shard, k in ((4, 4, far), (2, 3, 1), (3, -3, -1), (0, 1, 1), (1, -1, -1)):
                copies[role] = x_copy(n, ch, role, rsend.at[n, shard_at(ch, shard)], k)
                copies[role].start()
        return copies

    def x_combine(p, ch, copies):
        n = p * CHUNKS + ch
        shard = nz * PARTS[ch] // nx
        if nx > 1:
            even = (p + ch) % 2 == 0
            copies[2].wait_recv()
            copies[3].wait_recv()
            copies[4].wait_recv()
            for i, k in ((0, 2), (1, -2)) if even else ((1, -2), (0, 2)):
                value = own[n, shard_at(ch, k)] + rrecv[n, 2 + i, :shard].astype(F32)
                if even == (i == 0):
                    value = value + rrecv[n, 4, :shard].astype(F32)
                xcomb[n, i, :shard] = value.astype(BF)
                copies[5 + i] = x_copy(n, ch, 5 + i, xcomb.at[n, i, pl.ds(0, shard)], k)
                copies[5 + i].start()

    def x_sum(p, ch, copies):
        n = p * CHUNKS + ch
        shard = nz * PARTS[ch] // nx
        value = own[n, shard_at(ch, 0)]
        for role in (0, 1, 5, 6) if nx > 1 else ():
            copies[role].wait_recv()
            value = value + rrecv[n, role, :shard].astype(F32)
        return value

    def act_view(a, ch, k):
        return acts.at[(a * CHUNKS + ch) * CORES + core, shard_at(ch, k)]

    def to_sibling(a, ch, k):
        n = a * CHUNKS + ch
        view = act_view(a, ch, -k)
        copy = remote(view, view, s_ss.at[n, k], s_rs.at[n, k], sibling)
        copy.start()
        return copy

    def gather_copy(a, ch, k, away, target):
        n = a * CHUNKS + ch
        view = act_view(a, ch, away)
        return remote(view, view, a_ss.at[n, k], a_rs.at[n, k], at_x(target + nx)[1])

    def activate(ch, scatters):
        gate_pre = x_sum(0, ch, scatters[0])
        up_pre = x_sum(1, ch, scatters[1])
        sigma = 1.0 / (1.0 + jnp.exp(-gate_pre))
        gate_factor = up_pre * sigma * (1.0 + gate_pre * (1.0 - sigma))
        up_factor = gate_pre * sigma
        hidden_grad = x_sum(2, ch, scatters[2])
        mine = shard_at(ch, 0)
        acts[ch * CORES + core, mine] = (hidden_grad * gate_factor).astype(BF)
        acts[(CHUNKS + ch) * CORES + core, mine] = (hidden_grad * up_factor).astype(BF)
        gathers = {}
        if nx > 1:
            for k in (2, nx - 2, 1, nx - 1):
                for a in range(2):
                    gathers[a, k] = gather_copy(a, ch, k, 0, k)
                    gathers[a, k].start()
        forwards = [to_sibling(a, ch, 0) for a in range(2)]
        return gathers, forwards

    def pass_on(ch, gathers, forwards):
        if nx == 1:
            return
        for k in (2, nx - 2):
            step = 1 if k == 2 else -1
            for a in range(2):
                gathers[a, k].wait_recv()
                if (a == 0) == (k == 2):
                    gathers[a, 4] = gather_copy(a, ch, 4, -2 * step, 2 * step)
                    gathers[a, 4].start()
                third = 3 if k == 2 else nx - 3
                gathers[a, third] = gather_copy(a, ch, third, -2 * step, step)
                gathers[a, third].start()
                forwards.append(to_sibling(a, ch, k))
        for k in (1, nx - 1, 3, nx - 3, 4):
            for a in range(2):
                gathers[a, k].wait_recv()
                forwards.append(to_sibling(a, ch, k))

    def give_back(ch, forwards):
        part = PARTS[ch]
        total = nz * part
        for copy in forwards:
            copy.wait_recv()
        value = None
        for a, w in ((0, w_gate), (1, w_up)):
            for c in range(CORES):
                act = acts[(a * CHUNKS + ch) * CORES + c, :total]
                term = mm_nt(act, w[:, c * half : (c + 1) * half])
                value = term if value is None else value + term
        back[ch, :total] = value.astype(BF)
        copies = {}
        for k in near_first(nz):
            t, device = at_z(k)
            copies[k] = remote(
                block(back, t, part, ch),
                block(zret, z, part, ch),
                b_ss.at[ch, k],
                b_rs.at[ch, k],
                device,
            )
            copies[k].start()
        at_mine = pl.ds(pl.multiple_of(z * part, 16), part)
        zret[ch, at_mine] = back[ch, at_mine]
        return copies

    starts = [sum(PARTS[:ch]) for ch in range(CHUNKS)]
    weights = ((0, w_gate), (0, w_up), (1, w_down_t))

    pack_rows(0, y_in)
    z_start(0, 0)
    pack_rows(1, y_gr)
    z_start(1, 0)
    z_pass(0, 0)
    cores = []
    scatters = [[] for _ in PARTS]
    gathers = [None] * CHUNKS
    forwards = [None] * CHUNKS
    z_back = []

    def scatter_forward(ch):
        if ch + 1 < CHUNKS:
            z_start(0, ch + 1)
        z_finish(0, ch)
        pair = [cores_send(p, ch, *weights[p]) for p in (0, 1)]
        z_pass(1, ch)
        if ch + 1 < CHUNKS:
            z_start(1, ch + 1)
        for p in (0, 1):
            scatters[ch].append(x_scatter(p, ch, *weights[p], pair[p]))
        cores.extend(pair)

    def scatter_down(ch):
        z_finish(1, ch)
        copy = cores_send(2, ch, *weights[2])
        if ch + 1 < CHUNKS:
            z_pass(0, ch + 1)
        x_combine(0, ch, scatters[ch][0])
        x_combine(1, ch, scatters[ch][1])
        scatters[ch].append(x_scatter(2, ch, *weights[2], copy))
        cores.append(copy)

    def gather(ch):
        gathers[ch], forwards[ch] = activate(ch, scatters[ch])

    for ch in range(CHUNKS):
        scatter_forward(ch)
        if ch > 0:
            gather(ch - 1)
        scatter_down(ch)
        if ch > 0:
            pass_on(ch - 1, gathers[ch - 1], forwards[ch - 1])
        x_combine(2, ch, scatters[ch][2])
        if ch > 0:
            z_back.append(give_back(ch - 1, forwards[ch - 1]))
    last = CHUNKS - 1
    gather(last)
    pass_on(last, gathers[last], forwards[last])
    z_back.append(give_back(last, forwards[last]))

    for a, grad in ((0, grad_gate), (1, grad_up)):
        for c in range(CORES):
            value = None
            for ch in range(CHUNKS):
                total = nz * PARTS[ch]
                term = mm_tn(rows[ch, :total], acts[(a * CHUNKS + ch) * CORES + c, :total])
                value = term if value is None else value + term
            grad[:, c * half : (c + 1) * half] = value.astype(BF)

    spread = None
    for ch in range(CHUNKS):
        arrived(z_back[ch])
        for g in range(groups):
            value = None
            for q in range(HSPLIT):
                part = PARTS[ch]
                first = (g * HSPLIT + q) * part
                term = zret[ch, first : first + part].astype(F32)
                value = term if value is None else value + term
            first = g * per_z + starts[ch]
            term = mm(unpack[:, first : first + part], value.astype(BF))
            spread = term if spread is None else spread + term
    yback[...] = spread.astype(BF)
    y_back = {}
    for k in near_first(ny):
        t, device = at_y(k)
        y_back[k] = remote(block(yback, t, blk), block(yret, y, blk), e_ss.at[k], e_rs.at[k], device)
        y_back[k].start()
    here = pl.ds(pl.multiple_of(y * blk, 16), blk)
    yret[here] = yback[here]
    arrived(y_back)
    in_grad_t[...] = mm_tn(yret[...], pick[...]).astype(BF)

    for a in range(2):
        for ch in range(CHUNKS):
            z_sent(a * CHUNKS + ch, ch)
    flat = [y_in, y_gr, y_back, *z_back, *gathers]
    for each in scatters:
        flat.extend(each)
    for copies in flat:
        for copy in copies.values():
            copy.wait_send()
    for copy in cores:
        copy.wait_send()
    for each in forwards:
        for copy in each:
            copy.wait_send()


def per_device(sizes, out_grad, inputs, expert_ids, gate_weights, w_gate, w_up, w_down):
    nx, ny, nz = sizes
    tokens, feature = out_grad.shape
    hidden = w_gate.shape[1]
    half = hidden // CORES
    groups = nz // HSPLIT
    slots = ny * groups * SLOT
    per_z = ny * CAP
    part = max(PARTS)
    total = nz * part
    shard = total // nx
    dma = pltpu.SemaphoreType.DMA
    vmem = pltpu.VMEM
    in_grad_t, grad_gate, grad_up = pl.pallas_call(
        functools.partial(kernel, sizes),
        out_shape=(
            jax.ShapeDtypeStruct((feature, tokens), BF),
            jax.ShapeDtypeStruct((feature, hidden), BF),
            jax.ShapeDtypeStruct((feature, hidden), BF),
        ),
        in_specs=[pl.BlockSpec(memory_space=vmem)] * 7,
        out_specs=(pl.BlockSpec(memory_space=vmem),) * 3,
        scratch_shapes=[
            vmem((slots, tokens), BF),
            vmem((2, slots, feature), BF),
            vmem((2, slots, feature), BF),
            vmem((2 * CHUNKS * groups, part, feature), BF),
            vmem((2 * CHUNKS, total, feature), BF),
            vmem((3 * CHUNKS, total, half), BF),
            vmem((3 * CHUNKS, total, half), BF),
            vmem((3 * CHUNKS, total, half), F32),
            vmem((3 * CHUNKS, total, half), BF),
            vmem((3 * CHUNKS, 7, shard, half), BF),
            vmem((3 * CHUNKS, 2, shard, half), BF),
            vmem((2 * CHUNKS * CORES, total, half), BF),
            vmem((CHUNKS, total, feature), BF),
            vmem((CHUNKS, total, feature), BF),
            vmem((slots, feature), BF),
            vmem((slots, feature), BF),
            dma((2, ny)),
            dma((2, ny)),
            dma((2 * CHUNKS, 8)),
            dma((2 * CHUNKS, nz)),
            dma((3 * CHUNKS,)),
            dma((3 * CHUNKS,)),
            dma((3 * CHUNKS, 7)),
            dma((3 * CHUNKS, 7)),
            dma((2 * CHUNKS, nx)),
            dma((2 * CHUNKS, nx)),
            dma((2 * CHUNKS, nx)),
            dma((2 * CHUNKS, nx)),
            dma((CHUNKS, nz)),
            dma((CHUNKS, nz)),
            dma((ny,)),
            dma((ny,)),
        ],
        compiler_params=pltpu.CompilerParams(
            collective_id=0, has_side_effects=True, vmem_limit_bytes=48 * 1024 * 1024
        ),
        cost_estimate=pl.CostEstimate(
            flops=14 * nz * per_z * feature * hidden, bytes_accessed=4_000_000, transcendentals=0
        ),
    )(out_grad.T, inputs.T, expert_ids.T, gate_weights.T, w_gate, w_up, w_down.T)
    return in_grad_t.T, grad_gate, grad_up


def solution(mesh, sizes=None):
    if sizes is None:
        ny, nz = grid_of(mesh.shape["expert"])
        sizes = (mesh.shape["dp"] // CORES, ny, nz)
    placed = (
        P("expert", "dp"),
        P("expert", "dp"),
        P("expert", None),
        P("expert", None),
        P("dp", "expert"),
        P("dp", "expert"),
        P("expert", "dp"),
    )
    return jax.shard_map(
        functools.partial(per_device, sizes),
        mesh=mesh,
        in_specs=placed,
        out_specs=(P("expert", "dp"), P("dp", "expert"), P("dp", "expert")),
        check_vma=False,
    )
```

time: 142 us -> 123 us (0.87)
  the two profiles are of different devices: /device:TPU:11 before, /device:TPU:113 now
where the time goes in v2:
time: 123 us; the launch traced here: 122 us
  Pallas kernels  113 us (92%)
  local copies, waits for them, and re-layouts  8.54 us (7%)
    pallas_call x1, Pallas kernels, per_device(): pl.pallas_call(functools.partial(kernel, sizes), out_shape=(jax.ShapeDtyp...  113 us
    unnamed x17, local copies, waits for them, and re-layouts  8.54 us

profile of v2, /device:TPU:113, one launch (start us, length us, event | category | flops | bytes accessed | tf_op | source)
XLA Modules:
  0.0 121.7 jit_solution(8264038570058710630)
XLA Ops:
  0.6 0.0 copy-start.5
  0.6 0.7 copy-done.5
  1.3 0.0 copy-start
  1.3 1.0 copy-done
  2.3 0.0 copy-start.1
  2.4 1.0 copy-done.1
  3.4 0.0 copy-start.2
  3.4 1.0 copy-done.2
  4.4 0.0 copy-start.3
  4.4 0.9 copy-done.3
  5.3 0.0 copy-start.4
  5.3 0.9 copy-done.4
  6.3 0.0 copy-start.6
  6.3 0.7 copy-done.6
  7.0 112.5 %shard_map.94 = (bf16[448,256]{1,0:T(8,128)(2,1)S(1)}, bf16[448,512]{1,0:T(8,128)(2,1)S(1)}, bf16[448,512]{1,0:T(8,128)(2,1)S(1)}) custom-call(bf16[448,256]{1,0:T(8,128)(2,1)S(1)} %bitcast.8, bf16[448,256]{1,0:T(8,128)(2,1)S(1)} %bitcast.9, s32[8,256]{1,0:T(8,128)S(1)} %bitcast.10, f32[8,256]{1,0:T(8,128)S(1)} %bitcast.11, bf16[448,512]{1,0:T(8,128)(2,1)S(1)} %copy-done, ...), custom_call_target="tpu_custom_call" | custom-call | flops 2466250752 | bytes 4000000 | tf_op jit(solution)/shard_map/pallas_call | solution.py:572
  119.5 0.7 copy.13
  120.2 0.8 copy.14
  121.0 0.8 copy.15
Async XLA Ops:
  0.6 0.7 copy-start.5
  1.3 1.0 copy-start
  2.3 1.0 copy-start.1
  3.4 1.0 copy-start.2
  4.4 0.9 copy-start.3
  5.3 0.9 copy-start.4
  6.3 0.7 copy-start.6

commit v3 on v2

--- a/solution.py
+++ b/solution.py
@@ -63,6 +63,19 @@
 
 def kernel(
     sizes,
+    out_grad_h,
+    inputs_h,
+    ids_h,
+    gates_h,
+    w_gate_h,
+    w_up_h,
+    w_down_h,
+    in_grad_h,
+    grad_gate_h,
+    grad_up_h,
+    in_grad_t,
+    grad_gate,
+    grad_up,
     out_grad_t,
     inputs_t,
     ids_t,
@@ -70,9 +83,6 @@
     w_gate,
     w_up,
     w_down_t,
-    in_grad_t,
-    grad_gate,
-    grad_up,
     pick,
     ysend,
     yrecv,
@@ -105,6 +115,7 @@
     b_rs,
     e_ss,
     e_rs,
+    l_s,
 ):
     nx, ny, nz = sizes
     groups = nz // HSPLIT
@@ -143,6 +154,19 @@
             device_id_type=pl.DeviceIdType.MESH,
         )
 
+    loads = {}
+    for name, (source, target) in dict(
+        ids=(ids_h, ids_t),
+        inputs=(inputs_h, inputs_t),
+        gates=(gates_h, gates_t),
+        out_grad=(out_grad_h, out_grad_t),
+        w_gate=(w_gate_h, w_gate),
+        w_up=(w_up_h, w_up),
+        w_down=(w_down_h, w_down_t),
+    ).items():
+        loads[name] = pltpu.make_async_copy(source, target, l_s.at[len(loads)])
+        loads[name].start()
+
     partners = (
         [at_y(k)[1] for k in range(1, ny)]
         + [at_z(k)[1] for k in range(1, nz)]
@@ -155,6 +179,8 @@
 
     expert = iota((128, tokens), 0)
     hits = jnp.zeros((128, tokens), F32)
+    loads["ids"].wait()
+    loads["gates"].wait()
     gate = jnp.zeros((128, tokens), F32)
     for k in range(ids_t.shape[0]):
         hit = ids_t[k : k + 1, :] == expert
@@ -188,6 +214,7 @@
             copies[k].start()
         return copies
 
+    loads["inputs"].wait()
     ysend[0] = mm_nt(picker_b, inputs_t[...]).astype(BF)
     pl.semaphore_wait(barrier, len(partners))
     y_in = y_copies(0)
@@ -197,16 +224,20 @@
     gate_3 = (rest - gate_2.astype(F32)).astype(BF)
     gate_rt = mm(expand, gate_1) + mm(expand, gate_2) + mm(expand, gate_3)
     scale = jnp.sum(picker * gate_rt, axis=1, keepdims=True)
+    loads["out_grad"].wait()
     ysend[1] = (scale * mm_nt(picker_b, out_grad_t[...])).astype(BF)
     y_gr = y_copies(1)
 
+    def turn(value):
+        return value % 2 * (ny // 2) + value // 2
+
     col = iota((groups * per_z, slots), 1)
-    seat = (col // SLOT % groups) * per_z + (col // blk) * CAP + col % SLOT
+    seat = (col // SLOT % groups) * per_z + turn(col // blk) * CAP + col % SLOT
     pack = jnp.where(
         jnp.logical_and(seat == iota((groups * per_z, slots), 0), col % SLOT < CAP), 1.0, 0.0
     ).astype(BF)
     row = iota((slots, groups * per_z), 0)
-    seat_t = (row // SLOT % groups) * per_z + (row // blk) * CAP + row % SLOT
+    seat_t = (row // SLOT % groups) * per_z + turn(row // blk) * CAP + row % SLOT
     unpack = jnp.where(
         jnp.logical_and(seat_t == iota((slots, groups * per_z), 1), row % SLOT < CAP), 1.0, 0.0
     ).astype(BF)
@@ -421,6 +452,10 @@
                 gathers[a, third] = gather_copy(a, ch, third, -2 * step, step)
                 gathers[a, third].start()
                 forwards.append(to_sibling(a, ch, k))
+
+    def pass_rest(ch, gathers, forwards):
+        if nx == 1:
+            return
         for k in (1, nx - 1, 3, nx - 3, 4):
             for a in range(2):
                 gathers[a, k].wait_recv()
@@ -461,6 +496,8 @@
     pack_rows(1, y_gr)
     z_start(1, 0)
     z_pass(0, 0)
+    for name in ("w_gate", "w_up", "w_down"):
+        loads[name].wait()
     cores = []
     scatters = [[] for _ in PARTS]
     gathers = [None] * CHUNKS
@@ -501,10 +538,12 @@
             pass_on(ch - 1, gathers[ch - 1], forwards[ch - 1])
         x_combine(2, ch, scatters[ch][2])
         if ch > 0:
+            pass_rest(ch - 1, gathers[ch - 1], forwards[ch - 1])
             z_back.append(give_back(ch - 1, forwards[ch - 1]))
     last = CHUNKS - 1
     gather(last)
     pass_on(last, gathers[last], forwards[last])
+    pass_rest(last, gathers[last], forwards[last])
     z_back.append(give_back(last, forwards[last]))
 
     for a, grad in ((0, grad_gate), (1, grad_up)):
@@ -516,33 +555,51 @@
                 value = term if value is None else value + term
             grad[:, c * half : (c + 1) * half] = value.astype(BF)
 
-    spread = None
+    stores = []
+    for source, target in ((grad_gate, grad_gate_h), (grad_up, grad_up_h)):
+        stores.append(pltpu.make_async_copy(source, target, l_s.at[len(loads) + len(stores)]))
+        stores[-1].start()
+    y_back = {}
+    for k in near_first(ny):
+        t, device = at_y(k)
+        y_back[k] = remote(block(yback, t, blk), block(yret, y, blk), e_ss.at[k], e_rs.at[k], device)
+
     for ch in range(CHUNKS):
         arrived(z_back[ch])
+        part = PARTS[ch]
+        spread = None
         for g in range(groups):
             value = None
             for q in range(HSPLIT):
-                part = PARTS[ch]
                 first = (g * HSPLIT + q) * part
                 term = zret[ch, first : first + part].astype(F32)
                 value = term if value is None else value + term
             first = g * per_z + starts[ch]
             term = mm(unpack[:, first : first + part], value.astype(BF))
             spread = term if spread is None else spread + term
-    yback[...] = spread.astype(BF)
-    y_back = {}
-    for k in near_first(ny):
-        t, device = at_y(k)
-        y_back[k] = remote(block(yback, t, blk), block(yret, y, blk), e_ss.at[k], e_rs.at[k], device)
-        y_back[k].start()
+        spread = spread.astype(BF)
+        for t in range(ch, ny, CHUNKS):
+            yback[t * blk : (t + 1) * blk] = spread[t * blk : (t + 1) * blk]
+
+        def step(parity):
+            for k in near_first(ny):
+                if (k + parity) % 2 == ch:
+                    y_back[k].start()
+
+        for parity in range(2):
+            pl.when(y % 2 == parity)(functools.partial(step, parity))
     here = pl.ds(pl.multiple_of(y * blk, 16), blk)
     yret[here] = yback[here]
     arrived(y_back)
     in_grad_t[...] = mm_tn(yret[...], pick[...]).astype(BF)
+    stores.append(pltpu.make_async_copy(in_grad_t, in_grad_h, l_s.at[len(loads) + len(stores)]))
+    stores[-1].start()
 
     for a in range(2):
         for ch in range(CHUNKS):
             z_sent(a * CHUNKS + ch, ch)
+    for copy in stores:
+        copy.wait()
     flat = [y_in, y_gr, y_back, *z_back, *gathers]
     for each in scatters:
         flat.extend(each)
@@ -576,9 +633,19 @@
             jax.ShapeDtypeStruct((feature, hidden), BF),
             jax.ShapeDtypeStruct((feature, hidden), BF),
         ),
-        in_specs=[pl.BlockSpec(memory_space=vmem)] * 7,
-        out_specs=(pl.BlockSpec(memory_space=vmem),) * 3,
+        in_specs=[pl.BlockSpec(memory_space=pltpu.HBM)] * 7,
+        out_specs=(pl.BlockSpec(memory_space=pltpu.HBM),) * 3,
         scratch_shapes=[
+            vmem((feature, tokens), BF),
+            vmem((feature, hidden), BF),
+            vmem((feature, hidden), BF),
+            vmem((feature, tokens), BF),
+            vmem((feature, tokens), BF),
+            vmem((expert_ids.shape[1], tokens), jnp.int32),
+            vmem((expert_ids.shape[1], tokens), F32),
+            vmem((feature, hidden), BF),
+            vmem((feature, hidden), BF),
+            vmem((feature, hidden), BF),
             vmem((slots, tokens), BF),
             vmem((2, slots, feature), BF),
             vmem((2, slots, feature), BF),
@@ -611,9 +678,10 @@
             dma((CHUNKS, nz)),
             dma((ny,)),
             dma((ny,)),
+            dma((10,)),
         ],
         compiler_params=pltpu.CompilerParams(
-            collective_id=0, has_side_effects=True, vmem_limit_bytes=48 * 1024 * 1024
+            collective_id=0, has_side_effects=True, vmem_limit_bytes=56 * 1024 * 1024
         ),
         cost_estimate=pl.CostEstimate(
             flops=14 * nz * per_z * feature * hidden, bytes_accessed=4_000_000, transcendentals=0

time: 123 us -> 115 us (0.935)
  local copies, waits for them, and re-layouts: 8.54 us -> 3.65 us
  Pallas kernels: 113 us -> 110 us
    unnamed x17 -> x7, local copies, waits for them, and re-layouts: 8.54 us -> 3.65 us
    pallas_call x1, Pallas kernels: 113 us -> 110 us  [per_device(): pl.pallas_call(functools.partial(kernel, sizes), out_shape=(jax.ShapeDtyp...]
where the time goes in v3:
time: 115 us
  Pallas kernels  110 us (96%)
  local copies, waits for them, and re-layouts  3.65 us (3%)
    pallas_call x1, Pallas kernels, per_device(): pl.pallas_call(functools.partial(kernel, sizes), out_shape=(jax.ShapeDtyp...  110 us
    unnamed x7, local copies, waits for them, and re-layouts  3.65 us

profile of v3, /device:TPU:113, one launch (start us, length us, event | category | flops | bytes accessed | tf_op | source)
XLA Modules:
  0.0 114.7 jit_solution(16236843255639521061)
XLA Ops:
  0.6 110.4 %shard_map.94 = (bf16[448,256]{1,0:T(8,128)(2,1)}, bf16[448,512]{1,0:T(8,128)(2,1)}, bf16[448,512]{1,0:T(8,128)(2,1)}) custom-call(bf16[448,256]{1,0:T(8,128)(2,1)} %bitcast.8, bf16[448,256]{1,0:T(8,128)(2,1)} %bitcast.9, s32[8,256]{1,0:T(8,128)} %bitcast.10, f32[8,256]{1,0:T(8,128)} %bitcast.11, bf16[448,512]{1,0:T(8,128)(2,1)} %w_gate_h.1, ...), custom_call_target="tpu_custom_call" | custom-call | flops 2466250752 | bytes 4000000 | tf_op jit(solution)/shard_map/pallas_call | solution.py:629
  111.0 0.0 copy-start.1
  111.0 1.7 %copy.13 = bf16[256,448]{0,1:T(8,128)(2,1)} copy(bf16[256,448]{0,1:T(8,128)(2,1)} %bitcast.6) | data formatting | bytes 458752
  112.7 0.0 copy-done.1
  112.7 0.0 copy-start
  112.7 0.8 copy.14
  113.5 0.4 copy-done
  113.9 0.8 copy.15
Async XLA Ops:
  111.0 1.7 %copy-start.1 = (bf16[448,512]{1,0:T(8,128)(2,1)S(1)}, bf16[448,512]{1,0:T(8,128)(2,1)}, u32[]{:S(2)}) copy-start(bf16[448,512]{1,0:T(8,128)(2,1)} %get-tuple-element.13) | copy-start | bytes 1376260
  112.7 1.2 %copy-start = (bf16[448,512]{1,0:T(8,128)(2,1)S(1)}, bf16[448,512]{1,0:T(8,128)(2,1)}, u32[]{:S(2)}) copy-start(bf16[448,512]{1,0:T(8,128)(2,1)} %get-tuple-element.14) | copy-start | bytes 1376260

commit v4 on v3

--- a/solution.py
+++ b/solution.py
@@ -27,6 +27,33 @@
 CORES = 2
 BF = jnp.bfloat16
 F32 = jnp.float32
+
+
+def relay_tags(at):
+    return list(dict.fromkeys(tag for tag, _ in Z_SECOND[at]))
+
+
+def back_sends(at):
+    plan = []
+    for relay in range(HSPLIT):
+        for j, (tag, to) in enumerate(Z_SECOND[relay]):
+            if to == at:
+                plan.append((tag, False, relay, 4 + j))
+    for home in range(HSPLIT):
+        for j, (other, to) in enumerate(Z_FIRST[home]):
+            tag = home + HSPLIT * other
+            if to == at and tag not in relay_tags(at):
+                plan.append((tag, other == 1, home, j))
+    return plan
+
+
+def back_relays(at):
+    plan = []
+    for tag in relay_tags(at):
+        parts = [j for j, (each, _) in enumerate(Z_SECOND[at]) if each == tag]
+        home, other = tag % HSPLIT, tag // HSPLIT
+        plan.append((tag, parts, other == 1, home, Z_FIRST[home].index((other, at))))
+    return plan
 
 
 def grid_of(devices):
@@ -97,6 +124,8 @@
     acts,
     back,
     zret,
+    zcomb,
+    zsum,
     yback,
     yret,
     y_ss,
@@ -473,20 +502,60 @@
                 term = mm_nt(act, w[:, c * half : (c + 1) * half])
                 value = term if value is None else value + term
         back[ch, :total] = value.astype(BF)
-        copies = {}
-        for k in near_first(nz):
-            t, device = at_z(k)
-            copies[k] = remote(
-                block(back, t, part, ch),
-                block(zret, z, part, ch),
-                b_ss.at[ch, k],
-                b_rs.at[ch, k],
-                device,
-            )
-            copies[k].start()
-        at_mine = pl.ds(pl.multiple_of(z * part, 16), part)
-        zret[ch, at_mine] = back[ch, at_mine]
-        return copies
+
+        def step(at):
+            for j, (tag, other, to, buffer) in enumerate(back_sends(at)):
+                b_copy(ch, block(back, z_source(tag), part, ch), j, buffer, other, to).start()
+
+        each_place(step)
+
+    def b_copy(ch, source, j, buffer, other, to):
+        where = zret.at[ch, buffer, pl.ds(0, PARTS[ch])]
+        return remote(source, where, b_ss.at[ch, j], b_rs.at[ch, buffer], z_device(other, to))
+
+    def b_arrival(ch, buffer):
+        b_copy(ch, zcomb.at[ch, 0, pl.ds(0, PARTS[ch])], 0, buffer, False, 0).wait_recv()
+
+    def back_block(ch, source):
+        part = PARTS[ch]
+        return back[ch, pl.ds(pl.multiple_of(source * part, 16), part)].astype(F32)
+
+    def pass_back(ch):
+        part = PARTS[ch]
+
+        def step(at):
+            first = len(back_sends(at))
+            for i, (tag, parts, other, to, buffer) in enumerate(back_relays(at)):
+                value = back_block(ch, z_source(tag))
+                for j in parts:
+                    b_arrival(ch, 4 + j)
+                    value = value + zret[ch, 4 + j, :part].astype(F32)
+                zcomb[ch, i, :part] = value.astype(BF)
+                source = zcomb.at[ch, i, pl.ds(0, part)]
+                b_copy(ch, source, first + i, buffer, other, to).start()
+
+        each_place(step)
+
+    def add_back(ch):
+        part = PARTS[ch]
+
+        def step(at):
+            sums = [back_block(ch, z), None]
+            for j, (other, _) in enumerate(Z_FIRST[at]):
+                b_arrival(ch, j)
+                term = zret[ch, j, :part].astype(F32)
+                sums[other] = term if sums[other] is None else sums[other] + term
+            zsum[ch * groups + zgroup, :part] = sums[0].astype(BF)
+            zsum[ch * groups + 1 - zgroup, :part] = sums[1].astype(BF)
+
+        each_place(step)
+
+    def back_sent(ch):
+        def step(at):
+            for j in range(len(back_sends(at)) + len(back_relays(at))):
+                b_copy(ch, zcomb.at[ch, 0, pl.ds(0, PARTS[ch])], j, 0, False, 0).wait_send()
+
+        each_place(step)
 
     starts = [sum(PARTS[:ch]) for ch in range(CHUNKS)]
     weights = ((0, w_gate), (0, w_up), (1, w_down_t))
@@ -502,7 +571,6 @@
     scatters = [[] for _ in PARTS]
     gathers = [None] * CHUNKS
     forwards = [None] * CHUNKS
-    z_back = []
 
     def scatter_forward(ch):
         if ch + 1 < CHUNKS:
@@ -539,12 +607,14 @@
         x_combine(2, ch, scatters[ch][2])
         if ch > 0:
             pass_rest(ch - 1, gathers[ch - 1], forwards[ch - 1])
-            z_back.append(give_back(ch - 1, forwards[ch - 1]))
+            give_back(ch - 1, forwards[ch - 1])
     last = CHUNKS - 1
     gather(last)
+    for ch in range(last):
+        pass_back(ch)
     pass_on(last, gathers[last], forwards[last])
     pass_rest(last, gathers[last], forwards[last])
-    z_back.append(give_back(last, forwards[last]))
+    give_back(last, forwards[last])
 
     for a, grad in ((0, grad_gate), (1, grad_up)):
         for c in range(CORES):
@@ -565,17 +635,14 @@
         y_back[k] = remote(block(yback, t, blk), block(yret, y, blk), e_ss.at[k], e_rs.at[k], device)
 
     for ch in range(CHUNKS):
-        arrived(z_back[ch])
+        if ch == last:
+            pass_back(ch)
+        add_back(ch)
         part = PARTS[ch]
         spread = None
         for g in range(groups):
-            value = None
-            for q in range(HSPLIT):
-                first = (g * HSPLIT + q) * part
-                term = zret[ch, first : first + part].astype(F32)
-                value = term if value is None else value + term
             first = g * per_z + starts[ch]
-            term = mm(unpack[:, first : first + part], value.astype(BF))
+            term = mm(unpack[:, first : first + part], zsum[ch * groups + g, :part])
             spread = term if spread is None else spread + term
         spread = spread.astype(BF)
         for t in range(ch, ny, CHUNKS):
@@ -600,7 +667,9 @@
             z_sent(a * CHUNKS + ch, ch)
     for copy in stores:
         copy.wait()
-    flat = [y_in, y_gr, y_back, *z_back, *gathers]
+    for ch in range(CHUNKS):
+        back_sent(ch)
+    flat = [y_in, y_gr, y_back, *gathers]
     for each in scatters:
         flat.extend(each)
     for copies in flat:
@@ -659,7 +728,9 @@
             vmem((3 * CHUNKS, 2, shard, half), BF),
             vmem((2 * CHUNKS * CORES, total, half), BF),
             vmem((CHUNKS, total, feature), BF),
-            vmem((CHUNKS, total, feature), BF),
+            vmem((CHUNKS, 8, part, feature), BF),
+            vmem((CHUNKS, 3, part, feature), BF),
+            vmem((CHUNKS * groups, part, feature), BF),
             vmem((slots, feature), BF),
             vmem((slots, feature), BF),
             dma((2, ny)),
@@ -674,8 +745,8 @@
             dma((2 * CHUNKS, nx)),
             dma((2 * CHUNKS, nx)),
             dma((2 * CHUNKS, nx)),
-            dma((CHUNKS, nz)),
-            dma((CHUNKS, nz)),
+            dma((CHUNKS, 8)),
+            dma((CHUNKS, 8)),
             dma((ny,)),
             dma((ny,)),
             dma((10,)),

time: 115 us -> 113 us (0.983); the launches traced: 115 us -> 111 us
  Pallas kernels: 110 us -> 107 us
    pallas_call x1, Pallas kernels: 110 us -> 107 us  [per_device(): pl.pallas_call(functools.partial(kernel, sizes), out_shape=(jax.ShapeDtyp...]
where the time goes in v4:
time: 113 us; the launch traced here: 111 us
  Pallas kernels  107 us (95%)
  local copies, waits for them, and re-layouts  3.65 us (3%)
    pallas_call x1, Pallas kernels, per_device(): pl.pallas_call(functools.partial(kernel, sizes), out_shape=(jax.ShapeDtyp...  107 us
    unnamed x7, local copies, waits for them, and re-layouts  3.65 us

profile of v4, /device:TPU:113, one launch (start us, length us, event | category | flops | bytes accessed | tf_op | source)
XLA Modules:
  0.0 111.0 jit_solution(3806265108890778350)
XLA Ops:
  0.6 106.7 %shard_map.94 = (bf16[448,256]{1,0:T(8,128)(2,1)}, bf16[448,512]{1,0:T(8,128)(2,1)}, bf16[448,512]{1,0:T(8,128)(2,1)}) custom-call(bf16[448,256]{1,0:T(8,128)(2,1)} %bitcast.8, bf16[448,256]{1,0:T(8,128)(2,1)} %bitcast.9, s32[8,256]{1,0:T(8,128)} %bitcast.10, f32[8,256]{1,0:T(8,128)} %bitcast.11, bf16[448,512]{1,0:T(8,128)(2,1)} %w_gate_h.1, ...), custom_call_target="tpu_custom_call" | custom-call | flops 2466250752 | bytes 4000000 | tf_op jit(solution)/shard_map/pallas_call | solution.py:698
  107.4 0.0 copy-start.1
  107.4 1.7 %copy.13 = bf16[256,448]{0,1:T(8,128)(2,1)} copy(bf16[256,448]{0,1:T(8,128)(2,1)} %bitcast.6) | data formatting | bytes 458752
  109.1 0.0 copy-done.1
  109.1 0.0 copy-start
  109.1 0.8 copy.14
  109.9 0.4 copy-done
  110.3 0.8 copy.15
Async XLA Ops:
  107.4 1.7 %copy-start.1 = (bf16[448,512]{1,0:T(8,128)(2,1)S(1)}, bf16[448,512]{1,0:T(8,128)(2,1)}, u32[]{:S(2)}) copy-start(bf16[448,512]{1,0:T(8,128)(2,1)} %get-tuple-element.13) | copy-start | bytes 1376260
  109.1 1.2 %copy-start = (bf16[448,512]{1,0:T(8,128)(2,1)S(1)}, bf16[448,512]{1,0:T(8,128)(2,1)}, u32[]{:S(2)}) copy-start(bf16[448,512]{1,0:T(8,128)(2,1)} %get-tuple-element.14) | copy-start | bytes 1376260

commit v5 on v4

--- a/solution.py
+++ b/solution.py
@@ -575,10 +575,12 @@
     def scatter_forward(ch):
         if ch + 1 < CHUNKS:
             z_start(0, ch + 1)
+        else:
+            z_pass(1, ch)
         z_finish(0, ch)
         pair = [cores_send(p, ch, *weights[p]) for p in (0, 1)]
-        z_pass(1, ch)
         if ch + 1 < CHUNKS:
+            z_pass(1, ch)
             z_start(1, ch + 1)
         for p in (0, 1):
             scatters[ch].append(x_scatter(p, ch, *weights[p], pair[p]))

time: 113 us -> 113 us (level); the launches traced: 111 us -> 112 us
    pallas_call x1, Pallas kernels: 107 us -> 108 us  [per_device(): pl.pallas_call(functools.partial(kernel, sizes), out_shape=(jax.ShapeDtyp...]
where the time goes in v5:
time: 113 us; the launch traced here: 112 us
  Pallas kernels  108 us (96%)
  local copies, waits for them, and re-layouts  3.65 us (3%)
    pallas_call x1, Pallas kernels, per_device(): pl.pallas_call(functools.partial(kernel, sizes), out_shape=(jax.ShapeDtyp...  108 us
    unnamed x7, local copies, waits for them, and re-layouts  3.65 us

profile of v5, /device:TPU:113, one launch (start us, length us, event | category | flops | bytes accessed | tf_op | source)
XLA Modules:
  0.0 112.3 jit_solution(10225864299869768455)
XLA Ops:
  0.6 108.0 %shard_map.94 = (bf16[448,256]{1,0:T(8,128)(2,1)}, bf16[448,512]{1,0:T(8,128)(2,1)}, bf16[448,512]{1,0:T(8,128)(2,1)}) custom-call(bf16[448,256]{1,0:T(8,128)(2,1)} %bitcast.8, bf16[448,256]{1,0:T(8,128)(2,1)} %bitcast.9, s32[8,256]{1,0:T(8,128)} %bitcast.10, f32[8,256]{1,0:T(8,128)} %bitcast.11, bf16[448,512]{1,0:T(8,128)(2,1)} %w_gate_h.1, ...), custom_call_target="tpu_custom_call" | custom-call | flops 2466250752 | bytes 4000000 | tf_op jit(solution)/shard_map/pallas_call | solution.py:700
  108.6 0.0 copy-start.1
  108.6 1.7 %copy.13 = bf16[256,448]{0,1:T(8,128)(2,1)} copy(bf16[256,448]{0,1:T(8,128)(2,1)} %bitcast.6) | data formatting | bytes 458752
  110.3 0.0 copy-done.1
  110.3 0.0 copy-start
  110.3 0.8 copy.14
  111.1 0.4 copy-done
  111.5 0.8 copy.15
Async XLA Ops:
  108.6 1.7 %copy-start.1 = (bf16[448,512]{1,0:T(8,128)(2,1)S(1)}, bf16[448,512]{1,0:T(8,128)(2,1)}, u32[]{:S(2)}) copy-start(bf16[448,512]{1,0:T(8,128)(2,1)} %get-tuple-element.13) | copy-start | bytes 1376260
  110.3 1.2 %copy-start = (bf16[448,512]{1,0:T(8,128)(2,1)S(1)}, bf16[448,512]{1,0:T(8,128)(2,1)}, u32[]{:S(2)}) copy-start(bf16[448,512]{1,0:T(8,128)(2,1)} %get-tuple-element.14) | copy-start | bytes 1376260
